TPU v7x, 256 devices: a whole 4x4x8 slice. The times are simulated.
256 devices in a mesh: gx: 16 (over y, x), gy: 16 (over z, core).
Axes of the slice: x: 4, y: 4, z: 8, core: 2. Of those that a mesh axis runs over, the one named last changes fastest.
Arguments:
- pressure: float32 [2, 2048, 2048], P(None, 'gx', 'gy'), may hold values from 0.5 to 1.5
- saturations: float32 [2, 2, 2048, 2048], P(None, None, 'gx', 'gy'), may hold values from 0.05 to 0.4
- old_mass: float32 [3, 2, 2048, 2048], P(None, None, 'gx', 'gy'), may hold values from 0 to 0.4
- pore_volume: float32 [2, 2048, 2048], P(None, 'gx', 'gy'), may hold values from 0.3 to 3
- transmissibility: float32 [3, 2, 2048, 2048], P(None, None, 'gx', 'gy'), may hold values from 0.3 to 3
- direction: float32 [3, 2, 2048, 2048], P(None, None, 'gx', 'gy'), may hold values from -6 to 6
- seg_pressure: float32 [512, 128], P('gx'), may hold values from 0.4 to 1.2
- seg_direction: float32 [512, 128], P('gx'), may hold values from -6 to 6
- perf_cell: int32 [512, 128], P('gx'), may hold values from 0 to 524287, as said below
- well_index: float32 [512, 128], P('gx'), may hold values from 0.2 to 2
- parent: int32 [512, 128], P('gx'), may hold values from 0 to 126, as said below
- seg_head: float32 [512, 128], P('gx'), may hold values from 0 to 0.3
- well_mode: int32 [512], P('gx'), may hold values from 0 to 1
- bhp_limit: float32 [512], P('gx'), may hold values from 0.3 to 0.8
- guide_rate: float32 [512], P('gx'), may hold values from 0.5 to 5
- group_of: int32 [512, 1], P('gx'), may hold values from 0 to 127
- group_target: float32 [128], replicated, may hold values from 200 to 800
Outputs:
- cell_residual: float32 [3, 2, 2048, 2048], P(None, None, 'gx', 'gy')
- cell_jvp: float32 [3, 2, 2048, 2048], P(None, None, 'gx', 'gy')
- seg_residual: float32 [512, 128], P(('gx', 'gy'))
- seg_jvp: float32 [512, 128], P(('gx', 'gy'))
- group_rates: float32 [3, 128], replicated
Inputs may be any that keep to these rules, and one draw needn't show every extreme that they name: perf_cell codes (layer * 128 + xl) * 2048 + row, with xl the column within the strip of 128 columns of the well's block of 32 wells. `parent`: segment 0 of every well names itself; every other segment names a segment of lower number. `group_of`: every group has at least one well.
All inputs are finite; a program needn't handle non-finite values.
Results may differ from a plain program's by a relative error of at most 0.0003.
Values sent between devices are 32-bit elements; how exact they have to be, the bound alone decides.
A program may use at most 128 MiB of HBM per device.

v0:
```python
import jax
import jax.numpy as jnp
from jax import lax
from jax.sharding import PartitionSpec as P

COMPRESS = (0.05, 0.2, 1.0)
VISCOSITY = (0.5, 1.0, 0.2)
DENSITY = (1.0, 0.8, 0.2)
ROCK_COMP = 0.01
GRAVITY = 0.05
UPWIND_WIDTH = 0.02
FRICTION = 0.002
RATE_SCALE = 0.1


def padded_2(x, sides, width):
    for axis, dim in sides:
        devices, length = (lax.axis_size(axis), x.shape[dim])
        up = [(i, (i + 1) % devices) for i in range(devices - 1)]
        down = [(j, i) for i, j in up]
        last = lax.slice_in_dim(x, length - width, length, axis=dim)
        first = lax.slice_in_dim(x, 0, width, axis=dim)
        before = lax.ppermute(last, axis, up)
        after = lax.ppermute(first, axis, down)
        x = jnp.concatenate([before, x, after], axis=dim)
    return x


def phase_props(press, water, gas):
    oil = 1.0 - water - gas
    satur = (water, oil, gas)
    rock = 1.0 + ROCK_COMP * (press - 1.0)
    mobility = []
    masses = []
    for phase in range(3):
        volume = jnp.exp(COMPRESS[phase] * (press - 1.0))
        mobility.append(satur[phase] * satur[phase] * volume / VISCOSITY[phase])
        masses.append(rock * satur[phase] * volume)
    return (jnp.stack(mobility), jnp.stack(masses))


def face_flux(press_in, press_out, mobil_in, mobil_out, trans, lift):
    fluxes = []
    for phase in range(3):
        potential = press_in - press_out + DENSITY[phase] * lift
        upwind = jax.nn.sigmoid(potential / UPWIND_WIDTH)
        fluxes.append(
            trans * (upwind * mobil_in[phase] + (1.0 - upwind) * mobil_out[phase]) * potential
        )
    return jnp.stack(fluxes)


def ancestry(parent):
    count = parent.shape[1]
    segment_ids = jnp.arange(count, dtype=jnp.int32)
    reach = (segment_ids[None, :, None] == segment_ids[None, None, :]) | (
        parent[:, None, :] == segment_ids[None, :, None]
    )
    reach = reach.astype(jnp.bfloat16)
    for level in range((count - 1).bit_length()):
        product = jnp.einsum("wsu,wut->wst", reach, reach, preferred_element_type=jnp.float32)
        reach = jnp.minimum(product, 1.0).astype(jnp.bfloat16)
    return reach.astype(jnp.float32)


def segment_terms(parent, seg_head, well_mode, bhp_limit, target):
    reach = ancestry(parent)

    def equations(total_vals, seg_vals):
        flow = jnp.einsum("wst,wt->ws", reach, total_vals, precision=lax.Precision.HIGHEST)
        above = jnp.take_along_axis(seg_vals, parent, axis=1)
        inner = seg_vals - above - seg_head - FRICTION * flow
        root = jnp.where(
            well_mode == 1, RATE_SCALE * (flow[:, 0] - target), seg_vals[:, 0] - bhp_limit
        )
        return inner.at[:, 0].set(root)

    return equations


def per_device(
    pressure,
    saturations,
    old_mass,
    pore_volume,
    transmissibility,
    direction,
    seg_pressure,
    seg_direction,
    perf_cell,
    well_index,
    parent,
    seg_head,
    well_mode,
    bhp_limit,
    guide_rate,
    group_of,
    group_target,
):
    layers, cols, rows = pressure.shape
    col_count = lax.axis_size("gx")
    row_count = lax.axis_size("gy")
    col_index = lax.axis_index("gx")
    row_index = lax.axis_index("gy")
    col_glob = col_index * cols + jnp.arange(cols, dtype=jnp.int32)
    row_glob = row_index * rows + jnp.arange(rows, dtype=jnp.int32)
    trans_cols = jnp.where(
        (col_glob == cols * col_count - 1)[None, :, None], 0.0, transmissibility[0]
    )
    trans_rows = jnp.where(
        (row_glob == rows * row_count - 1)[None, None, :], 0.0, transmissibility[1]
    )
    stacked = jnp.concatenate(
        [pressure[None], saturations, direction, trans_cols[None], trans_rows[None]], axis=0
    )
    padded = padded_2(stacked, (("gx", 2), ("gy", 3)), 1)
    state_pad = padded[0:3]
    direc_pad = padded[3:6]
    tcol_pad = padded[6]
    trow_pad = padded[7]
    all_rows = rows * row_count
    layer_span = cols * all_rows
    layer = perf_cell // layer_span
    remain = perf_cell % layer_span
    local_row = remain % all_rows - row_index * rows
    owned = (local_row >= 0) & (local_row < rows)
    flat_cell = (layer * cols + remain // all_rows) * rows + jnp.clip(local_row, 0, rows - 1)
    weight = jnp.where(owned, well_index, 0.0)

    def local_terms(state, seg_vals):
        press = state[0]
        mobility, masses = phase_props(press, state[1], state[2])
        mobil_in = mobility[:, :, 1:-1, 1:-1]
        press_in = press[:, 1:-1, 1:-1]
        residual = masses[:, :, 1:-1, 1:-1] * pore_volume - old_mass
        flux_cols = face_flux(
            press[:, :-1, 1:-1],
            press[:, 1:, 1:-1],
            mobility[:, :, :-1, 1:-1],
            mobility[:, :, 1:, 1:-1],
            tcol_pad[:, :-1, 1:-1],
            0.0,
        )
        residual = residual + flux_cols[:, :, 1:] - flux_cols[:, :, :-1]
        flux_rows = face_flux(
            press[:, 1:-1, :-1],
            press[:, 1:-1, 1:],
            mobility[:, :, 1:-1, :-1],
            mobility[:, :, 1:-1, 1:],
            trow_pad[:, 1:-1, :-1],
            0.0,
        )
        residual = residual + flux_rows[:, :, :, 1:] - flux_rows[:, :, :, :-1]
        flux_layers = face_flux(
            press_in[:-1],
            press_in[1:],
            mobil_in[:, :-1],
            mobil_in[:, 1:],
            transmissibility[2][:-1],
            GRAVITY,
        )
        residual = (
            residual
            + jnp.pad(flux_layers, ((0, 0), (0, 1), (0, 0), (0, 0)))
            - jnp.pad(flux_layers, ((0, 0), (1, 0), (0, 0), (0, 0)))
        )
        mobil_flat = mobil_in.reshape(3, -1)
        rates = weight * mobil_flat[:, flat_cell] * (press_in.reshape(-1)[flat_cell] - seg_vals)
        residual = (
            residual.reshape(3, -1)
            .at[:, flat_cell.reshape(-1)]
            .add(rates.reshape(3, -1))
            .reshape(residual.shape)
        )
        return (residual, rates)

    primal, tangent = jax.jvp(local_terms, (state_pad, seg_pressure), (direc_pad, seg_direction))
    cell_residual, rates = primal
    cell_jvp, rate_tangent = tangent
    rate_total = jnp.sum(rates, axis=0)
    total_tangent = jnp.sum(rate_tangent, axis=0)
    member = (
        group_of[:, 0][:, None] == jnp.arange(group_target.shape[0], dtype=jnp.int32)[None, :]
    ).astype(jnp.float32)
    rates_part = jnp.dot(jnp.sum(rates, axis=2), member, precision=lax.Precision.HIGHEST)
    guide_part = jnp.dot(guide_rate, member, precision=lax.Precision.HIGHEST)
    guide_total = lax.psum(guide_part, "gx")
    group_rates = lax.psum(rates_part, ("gx", "gy"))
    target = (
        jnp.dot(member, group_target, precision=lax.Precision.HIGHEST)
        * guide_rate
        / jnp.dot(member, guide_total, precision=lax.Precision.HIGHEST)
    )
    well_count = seg_pressure.shape[0]
    share = well_count // row_count
    start = row_index * share

    def pick(values):
        return lax.dynamic_slice_in_dim(values, start, share, 0)

    total_sum, tangent_sum = lax.psum((rate_total, total_tangent), "gy")
    equations = segment_terms(parent, seg_head, well_mode, bhp_limit, target)
    seg_full, seg_tan = jax.jvp(equations, (total_sum, seg_pressure), (tangent_sum, seg_direction))
    seg_residual = pick(seg_full)
    seg_jvp = pick(seg_tan)
    return (cell_residual, cell_jvp, seg_residual, seg_jvp, group_rates)


def solution(mesh):
    placed = (
        P(None, "gx", "gy"),
        P(None, None, "gx", "gy"),
        P(None, None, "gx", "gy"),
        P(None, "gx", "gy"),
        P(None, None, "gx", "gy"),
        P(None, None, "gx", "gy"),
        P("gx", None),
        P("gx", None),
        P("gx", None),
        P("gx", None),
        P("gx", None),
        P("gx", None),
        P("gx"),
        P("gx"),
        P("gx"),
        P("gx", None),
        P(),
    )
    return jax.shard_map(
        per_device,
        mesh=mesh,
        in_specs=placed,
        out_specs=(
            P(None, None, "gx", "gy"),
            P(None, None, "gx", "gy"),
            P(("gx", "gy"), None),
            P(("gx", "gy"), None),
            P(),
        ),
        check_vma=False,
    )
```

profile of v0, /device:TPU:1, one launch (start us, length us, event | category | flops | bytes accessed | tf_op | source)
XLA Modules:
  0.0 510.7 jit_solution(14686973665699037031)
XLA Ops:
  6.9 4.6 collective-permute-start
  15.0 2.0 minimum_convert_fusion
  17.2 32.3 %psum.29 = f32[128]{0:T(128)S(1)} all-reduce(f32[128]{0:T(128)S(1)} %convolution_bitcast_fusion.1), channel_id=1, replica_groups=mesh['gx'=16,'gy'=16] {'gx'}, use_global_device_ids=true, to_apply=%region_5.6 | all-reduce | flops 128 | bytes 1024 | tf_op jit(solution)/shard_map/psum | solution.py:187
  51.9 9.9 %collective-permute-start.3 = (f32[8,2,130,1]{2,0,3,1:T(8,128)S(1)}, f32[8,2,130,1]{2,0,3,1:T(8,128)S(1)}, u32[]{:S(2)}, u32[]{:S(2)}) collective-permute-start(f32[8,2,130,1]{2,0,3,1:T(8,128)S(1)} %copy.106), channel_id=1, source_target_pairs={{1,0},{2,1},{3,2},{4,3},{5,4},{6,5},{7,6},{8,7},{9,8},{10,9},{11,1... | collective-permute-start | bytes 24968 | tf_op jit(solution)/shard_map/ppermute | solution.py:24
  62.4 3.6 collective-permute-start.2
  66.2 43.2 %gather_fusion.5 = f32[4096]{0:T(1024)} fusion(f32[32,128]{1,0:T(8,128)S(1)} %copy-done.1, s32[4096]{0:T(1024)S(1)} %fusion.156), kind=kCustom, calls=%fused_computation.5 | custom fusion | bytes 65536 | tf_op jit(solution)/shard_map/jvp(jit(take_along_axis))/gather | solution.py:71
  109.4 25.6 %gather_fusion.4 = f32[4096]{0:T(1024)S(1)} fusion(f32[32,128]{1,0:T(8,128)S(1)} %copy-done.2, s32[4096]{0:T(1024)S(1)} %fusion.156), kind=kCustom, calls=%fused_computation.4 | custom fusion | bytes 65536 | tf_op jit(solution)/shard_map/jvp(jit(take_along_axis))/gather | solution.py:71
  145.2 8.6 %copy.109 = f32[3,2,128,128]{0,3,2,1:T(8,128)} copy(f32[3,2,128,128]{3,2,1,0:T(8,128)S(1)} %fusion.34) | data formatting | bytes 786432 | tf_op jit(solution)/shard_map/jvp()/sub | solution.py:163
  153.7 8.5 %copy.110 = f32[3,2,128,128]{0,3,2,1:T(8,128)} copy(f32[3,2,128,128]{3,2,1,0:T(8,128)S(1)} %get-tuple-element.106) | data formatting | bytes 786432 | tf_op jit(solution)/shard_map/jvp()/slice | solution.py:133
  162.2 16.5 %gather_fusion = f32[4096,3]{1,0:T(8,128)S(1)} fusion(f32[3,32768]{0,1:T(8,128)} %bitcast.414, s32[4096]{0:T(1024)S(1)} %get-tuple-element.69), kind=kCustom, calls=%fused_computation | custom fusion | bytes 114688 | tf_op jit(solution)/shard_map/jvp()/gather | solution.py:168
  178.8 40.6 %gather_fusion.3 = f32[4096]{0:T(1024)} fusion(f32[32768]{0:T(1024)S(1)} %bitcast.407, s32[4096]{0:T(1024)S(1)} %get-tuple-element.69), kind=kCustom, calls=%fused_computation.3 | custom fusion | bytes 49152 | tf_op jit(solution)/shard_map/jvp()/gather | solution.py:168
  219.4 23.0 %gather_fusion.1 = f32[4096]{0:T(1024)S(1)} fusion(f32[32768]{0:T(1024)S(1)} %bitcast.408, s32[4096]{0:T(1024)S(1)} %get-tuple-element.69), kind=kCustom, calls=%fused_computation.1 | custom fusion | bytes 49152 | tf_op jit(solution)/shard_map/jvp()/gather | solution.py:168
  242.4 36.5 %scatter_custom_fusion = f32[3,32768]{0,1:T(8,128)} fusion(f32[3,32768]{0,1:T(8,128)} %bitcast.409, s32[4096]{0:T(1024)} %bitcast.429, f32[4096,3]{1,0:T(8,128)S(1)} %gather_fusion, f32[4096]{0:T(1024)S(1)} %bitcast.419, f32[4096]{0:T(1024)S(1)} %bitcast.417), kind=kCustom, calls=%fused_computation.15 | custom fusion | flops 36864 | bytes 475136 | tf_op jit(solution)/shard_map/jvp()/scatter-add | solution.py:172
  278.9 10.7 %copy.115 = f32[3,2,128,128]{3,2,1,0:T(8,128)} copy(f32[3,2,128,128]{0,3,2,1:T(8,128)} %bitcast.410) | data formatting | bytes 786432
  289.6 2.5 fusion.31
  292.1 9.5 %copy.111 = f32[3,2,128,128]{0,3,2,1:T(8,128)} copy(f32[3,2,128,128]{3,2,1,0:T(8,128)} %fusion.31) | data formatting | bytes 786432 | tf_op jit(solution)/shard_map/jvp()/sub | solution.py:163
  301.6 8.5 %copy.112 = f32[3,2,128,128]{0,3,2,1:T(8,128)} copy(f32[3,2,128,128]{3,2,1,0:T(8,128)S(1)} %get-tuple-element.105) | data formatting | bytes 786432 | tf_op jit(solution)/shard_map/jvp()/slice | solution.py:133
  310.1 19.9 %gather_fusion.2 = f32[4096,3]{1,0:T(8,128)} fusion(f32[3,32768]{0,1:T(8,128)} %bitcast.415, s32[4096]{0:T(1024)S(1)} %get-tuple-element.69), kind=kCustom, calls=%fused_computation.2 | custom fusion | bytes 114688 | tf_op jit(solution)/shard_map/jvp()/gather | solution.py:168
  330.1 37.0 %scatter_custom_fusion.1 = f32[3,32768]{0,1:T(8,128)} fusion(f32[3,32768]{0,1:T(8,128)} %bitcast.411, s32[4096]{0:T(1024)} %bitcast.430, f32[4096,3]{1,0:T(8,128)} %gather_fusion.2, f32[4096,3]{1,0:T(8,128)S(1)} %gather_fusion, f32[4096]{0:T(1024)S(1)} %bitcast.425, f32[4096]{0:T(1024)S(1)} %bitcast.420, f32[4096]{0:T(1024)S(1)} %bitcast.418), kind=kCustom, calls=%fused_computation.13 | custom fusion | flops 73728 | bytes 2588672 | tf_op jit(solution)/shard_map/jvp()/scatter-add | solution.py:172
  367.0 10.6 %copy.116 = f32[3,2,128,128]{3,2,1,0:T(8,128)} copy(f32[3,2,128,128]{0,3,2,1:T(8,128)} %bitcast.412) | data formatting | bytes 786432
  377.7 4.6 add_reduce_fusion
  382.4 46.0 %all-reduce.4 = (f32[32,128]{1,0:T(8,128)S(1)}, f32[32,128]{1,0:T(8,128)S(1)}) all-reduce(f32[32,128]{1,0:T(8,128)S(1)} %get-tuple-element.55, f32[32,128]{1,0:T(8,128)S(1)} %get-tuple-element.54), channel_id=1, replica_groups=mesh['gx'=16,'gy'=16] {'gy'}, use_global_device_ids=true, to_apply=%region_3.4 | all-reduce | flops 8192 | bytes 65536 | tf_op jit(solution)/shard_map/psum | solution.py:201
  430.2 1.7 fusion.174
  435.5 75.3 %psum.31 = f32[3,128]{1,0:T(4,128)} all-reduce(f32[3,128]{1,0:T(4,128)S(1)} %fusion.157), channel_id=1, replica_groups=mesh['gx'=16,'gy'=16] {'gx','gy'}, use_global_device_ids=true, to_apply=%region_9.10 | all-reduce | flops 384 | bytes 3072 | tf_op jit(solution)/shard_map/psum | solution.py:188
  (113 shorter events, 28.2 us)
Async XLA Ops:
  0.6 431.5 %copy-start = (f32[128]{0:T(128)S(1)}, f32[128]{0:T(128)}, u32[]{:S(2)}) copy-start(f32[128]{0:T(128)} %param.37) | copy-start | bytes 1540
  0.6 10.9 %copy-start.8 = (s32[32,128]{1,0:T(8,128)S(1)}, s32[32,128]{1,0:T(8,128)}, u32[]{:S(2)}) copy-start(s32[32,128]{1,0:T(8,128)} %param.29) | copy-start | bytes 49156
  0.7 11.5 %copy-start.12 = (f32[32,128]{1,0:T(8,128)S(1)}, f32[32,128]{1,0:T(8,128)}, u32[]{:S(2)}) copy-start(f32[32,128]{1,0:T(8,128)} %param.30) | copy-start | bytes 49156
  0.7 11.5 %copy-start.9 = (s32[32,128]{1,0:T(8,128)S(1)}, s32[32,128]{1,0:T(8,128)}, u32[]{:S(2)}) copy-start(s32[32,128]{1,0:T(8,128)} %param.31) | copy-start | bytes 49156
  5.6 45.2 %collective-permute-start.1 = (f32[8,2,1,128]{3,2,1,0:T(1,128)S(1)}, f32[8,2,1,128]{3,2,1,0:T(1,128)S(1)}, u32[]{:S(2)}, u32[]{:S(2)}) collective-permute-start(f32[8,2,1,128]{3,2,1,0:T(1,128)S(1)} %get-tuple-element.89), channel_id=1, source_target_pairs={{16,0},{32,16},{48,32},{64,48},{80,64},{96,80},{112,96},{128,112},... | collective-permute-start | bytes 24584 | tf_op jit(solution)/shard_map/ppermute | solution.py:24
  6.9 43.9 %collective-permute-start = (f32[8,2,1,128]{3,2,1,0:T(1,128)S(1)}, f32[8,2,1,128]{3,2,1,0:T(1,128)S(1)}, u32[]{:S(2)}, u32[]{:S(2)}) collective-permute-start(f32[8,2,1,128]{3,2,1,0:T(1,128)S(1)} %get-tuple-element.88), channel_id=1, source_target_pairs={{0,16},{16,32},{32,48},{48,64},{64,80},{80,96},{96,112},{112,128},... | collective-permute-start | bytes 24584 | tf_op jit(solution)/shard_map/ppermute | solution.py:23
  15.0 2.0 copy-start.16
  15.0 2.0 copy-start.19
  15.0 35.2 %copy-start.2 = (f32[32,128]{1,0:T(8,128)S(1)}, f32[32,128]{1,0:T(8,128)}, u32[]{:S(2)}) copy-start(f32[32,128]{1,0:T(8,128)} %param.27) | copy-start | bytes 49156
  51.3 14.8 %copy-start.1 = (f32[32,128]{1,0:T(8,128)S(1)}, f32[32,128]{1,0:T(8,128)}, u32[]{:S(2)}) copy-start(f32[32,128]{1,0:T(8,128)} %param.28) | copy-start | bytes 49156
  51.9 83.8 %collective-permute-start.3 = (f32[8,2,130,1]{2,0,3,1:T(8,128)S(1)}, f32[8,2,130,1]{2,0,3,1:T(8,128)S(1)}, u32[]{:S(2)}, u32[]{:S(2)}) collective-permute-start(f32[8,2,130,1]{2,0,3,1:T(8,128)S(1)} %copy.106), channel_id=1, source_target_pairs={{1,0},{2,1},{3,2},{4,3},{5,4},{6,5},{7,6},{8,7},{9,8},{10,9},{11,1... | collective-permute-start | bytes 24968 | tf_op jit(solution)/shard_map/ppermute | solution.py:24
  62.4 73.7 %collective-permute-start.2 = (f32[8,2,130,1]{2,0,3,1:T(8,128)S(1)}, f32[8,2,130,1]{2,0,3,1:T(8,128)S(1)}, u32[]{:S(2)}, u32[]{:S(2)}) collective-permute-start(f32[8,2,130,1]{2,0,3,1:T(8,128)S(1)} %copy.105), channel_id=1, source_target_pairs={{0,1},{1,2},{2,3},{3,4},{4,5},{5,6},{6,7},{7,8},{8,9},{9,10},{10,1... | collective-permute-start | bytes 24968 | tf_op jit(solution)/shard_map/ppermute | solution.py:23
  143.0 1.8 copy-start.6
  219.4 23.0 %copy-start.11 = (f32[4096]{0:T(1024)S(1)}, f32[4096]{0:T(1024)}, u32[]{:S(2)}) copy-start(f32[4096]{0:T(1024)} %gather_fusion.3) | copy-start | bytes 49156
  278.9 10.7 %copy-start.4 = (f32[3,1,128,128]{3,2,1,0:T(8,128)S(1)}, f32[3,1,128,128]{3,2,1,0:T(8,128)}, u32[]{:S(2)}) copy-start(f32[3,1,128,128]{3,2,1,0:T(8,128)} %get-tuple-element.112) | copy-start | bytes 589828
  377.7 50.7 %copy-start.3 = (bf16[32,128,128]{2,1,0:T(8,128)(2,1)S(1)}, bf16[32,128,128]{2,1,0:T(8,128)(2,1)}, u32[]{:S(2)}) copy-start(bf16[32,128,128]{2,1,0:T(8,128)(2,1)} %minimum_convert_fusion) | copy-start | bytes 3145732
  377.7 52.5 %copy-start.10 = (f32[4096]{0:T(1024)S(1)}, f32[4096]{0:T(1024)}, u32[]{:S(2)}) copy-start(f32[4096]{0:T(1024)} %gather_fusion.5) | copy-start | bytes 49156
  382.3 49.8 %copy-start.14 = (f32[32]{0:T(128)S(1)}, f32[32]{0:T(128)}, u32[]{:S(2)}) copy-start(f32[32]{0:T(128)} %slice_reduce_fusion.2) | copy-start | bytes 388
  382.3 49.8 %copy-start.15 = (s32[32]{0:T(128)S(1)}, s32[32]{0:T(128)}, u32[]{:S(2)}) copy-start(s32[32]{0:T(128)} %param.33) | copy-start | bytes 388
  382.3 49.8 %copy-start.17 = (f32[32]{0:T(128)S(1)}, f32[32]{0:T(128)}, u32[]{:S(2)}) copy-start(f32[32]{0:T(128)} %param.35) | copy-start | bytes 388
  382.3 49.8 %copy-start.18 = (f32[32]{0:T(128)S(1)}, f32[32]{0:T(128)}, u32[]{:S(2)}) copy-start(f32[32]{0:T(128)} %param.34) | copy-start | bytes 388
  382.4 49.8 %copy-start.20 = (s32[32,1]{0,1:T(1,128)S(1)}, s32[32,1]{0,1:T(1,128)}, u32[]{:S(2)}) copy-start(s32[32,1]{0,1:T(1,128)} %param.36) | copy-start | bytes 388
  382.4 49.8 %copy-start.21 = (f32[32]{0:T(128)S(1)}, f32[32]{0:T(128)}, u32[]{:S(2)}) copy-start(f32[32]{0:T(128)} %convolution_bitcast_fusion) | copy-start | bytes 388
  382.4 50.1 %copy-start.13 = (f32[32,128]{1,0:T(8,128)S(1)}, f32[32,128]{1,0:T(8,128)}, u32[]{:S(2)}) copy-start(f32[32,128]{1,0:T(8,128)} %param.32) | copy-start | bytes 49156
  (2 other events, 3.0 us)
where the time goes:
time: 512 us; the launch traced here: 511 us
  local copies, waits for them, and re-layouts  233 us (46%)
  blocking collectives  154 us (30%)
  other arithmetic  93.7 us (18%)
  starting transfers between devices  19.4 us (4%)
  matrix products  9.4 us (2%)
    psum x1, blocking collectives, per_device(): group_rates = lax.psum(rates_part, ('gx', 'gy'))  75.3 us
    scatter-add x2, other arithmetic, local_terms(): residual = residual.reshape(3, -1).at[:, flat_cell.reshape(-1)].add(rates...  73.5 us
    gather x2, local copies, waits for them, and re-layouts, equations(): above = jnp.take_along_axis(seg_vals, parent, axis=1)  68.8 us
    gather x2, local copies, waits for them, and re-layouts, local_terms(): press_in.reshape(-1)[flat_cell] - seg_vals  63.6 us
    psum x1, blocking collectives, per_device(): total_sum, tangent_sum = lax.psum((rate_total, total_tangent), 'gy')  46 us
    gather x2, local copies, waits for them, and re-layouts, local_terms(): mobil_flat[:, flat_cell]  36.5 us
    psum x1, blocking collectives, per_device(): guide_total = lax.psum(guide_part, 'gx')  32.3 us
    unnamed x49, local copies, waits for them, and re-layouts  24.4 us
  transfers between devices with their start and end apart: 4, of which 0 were waited for; matrix products, arithmetic and copies ran while one was open for 15% of the time, Pallas kernels for 0%

commit v1 on v0

--- a/solution.py
+++ b/solution.py
@@ -185,7 +185,7 @@
     rates_part = jnp.dot(jnp.sum(rates, axis=2), member, precision=lax.Precision.HIGHEST)
     guide_part = jnp.dot(guide_rate, member, precision=lax.Precision.HIGHEST)
     guide_total = lax.psum(guide_part, "gx")
-    group_rates = lax.psum(rates_part, ("gx", "gy"))
+    group_rates = lax.psum(lax.psum(rates_part, "gy"), "gx")
     target = (
         jnp.dot(member, group_target, precision=lax.Precision.HIGHEST)
         * guide_rate

time: 512 us -> 437 us (0.85); the launches traced: 511 us -> 429 us
  blocking collectives: 154 us -> 78 us
  starting transfers between devices: 19.4 us -> 13.1 us
    psum x1 -> x0, blocking collectives: 75.3 us -> none  [per_device(): group_rates = lax.psum(rates_part, ('gx', 'gy'))]
  transfers between devices with their start and end apart: 4 -> 4, of which waited for: 0 -> 0; matrix products, arithmetic and copies ran while one was open for 15% -> 18% of each run, Pallas kernels for 0% -> 0%
where the time goes in v1:
time: 437 us; the launch traced here: 429 us
  local copies, waits for them, and re-layouts  234 us (54%)
  other arithmetic  93.7 us (21%)
  blocking collectives  78 us (18%)
  starting transfers between devices  13.1 us (3%)
  matrix products  9.38 us (2%)
    scatter-add x2, other arithmetic, local_terms(): residual = residual.reshape(3, -1).at[:, flat_cell.reshape(-1)].add(rates...  73.5 us
    gather x2, local copies, waits for them, and re-layouts, equations(): above = jnp.take_along_axis(seg_vals, parent, axis=1)  68.8 us
    gather x2, local copies, waits for them, and re-layouts, local_terms(): press_in.reshape(-1)[flat_cell] - seg_vals  63.6 us
    psum x1, blocking collectives, per_device(): total_sum, tangent_sum = lax.psum((rate_total, total_tangent), 'gy')  45.6 us
    gather x2, local copies, waits for them, and re-layouts, local_terms(): mobil_flat[:, flat_cell]  36.5 us
    psum x1, blocking collectives, per_device(): guide_total = lax.psum(guide_part, 'gx')  32.3 us
    unnamed x49, local copies, waits for them, and re-layouts  24.4 us
    sub x2, local copies, waits for them, and re-layouts, local_terms(): residual + jnp.pad(flux_layers, ((0, 0), (0, 1), (0, 0), (0, 0)))  18.1 us
  transfers between devices with their start and end apart: 4, of which 0 were waited for; matrix products, arithmetic and copies ran while one was open for 18% of the time, Pallas kernels for 0%

profile of v1, /device:TPU:1, one launch (start us, length us, event | category | flops | bytes accessed | tf_op | source)
XLA Modules:
  0.0 428.9 jit_solution(16992147838126183002)
XLA Ops:
  6.9 4.6 %collective-permute-start = (f32[8,2,1,128]{3,2,1,0:T(1,128)S(1)}, f32[8,2,1,128]{3,2,1,0:T(1,128)S(1)}, u32[]{:S(2)}, u32[]{:S(2)}) collective-permute-start(f32[8,2,1,128]{3,2,1,0:T(1,128)S(1)} %get-tuple-element.91), channel_id=1, source_target_pairs={{0,16},{16,32},{32,48},{48,64},{64,80},{80,96},{96,112},{112,128},... | collective-permute-start | bytes 24584 | tf_op jit(solution)/shard_map/ppermute | solution.py:23
  15.0 2.0 minimum_convert_fusion
  19.4 5.1 %collective-permute-start.3 = (f32[8,2,130,1]{2,0,3,1:T(8,128)S(1)}, f32[8,2,130,1]{2,0,3,1:T(8,128)S(1)}, u32[]{:S(2)}, u32[]{:S(2)}) collective-permute-start(f32[8,2,130,1]{2,0,3,1:T(8,128)S(1)} %copy.106), channel_id=1, source_target_pairs={{1,0},{2,1},{3,2},{4,3},{5,4},{6,5},{7,6},{8,7},{9,8},{10,9},{11,1... | collective-permute-start | bytes 24968 | tf_op jit(solution)/shard_map/ppermute | solution.py:24
  25.1 2.1 collective-permute-start.2
  27.4 43.2 %gather_fusion.5 = f32[4096]{0:T(1024)} fusion(f32[32,128]{1,0:T(8,128)S(1)} %copy-done.1, s32[4096]{0:T(1024)S(1)} %fusion.156), kind=kCustom, calls=%fused_computation.5 | custom fusion | bytes 65536 | tf_op jit(solution)/shard_map/jvp(jit(take_along_axis))/gather | solution.py:71
  70.5 25.6 %gather_fusion.4 = f32[4096]{0:T(1024)S(1)} fusion(f32[32,128]{1,0:T(8,128)S(1)} %copy-done.2, s32[4096]{0:T(1024)S(1)} %fusion.156), kind=kCustom, calls=%fused_computation.4 | custom fusion | bytes 65536 | tf_op jit(solution)/shard_map/jvp(jit(take_along_axis))/gather | solution.py:71
  106.4 8.6 %copy.109 = f32[3,2,128,128]{0,3,2,1:T(8,128)} copy(f32[3,2,128,128]{3,2,1,0:T(8,128)S(1)} %fusion.34) | data formatting | bytes 786432 | tf_op jit(solution)/shard_map/jvp()/sub | solution.py:163
  114.9 8.6 %copy.110 = f32[3,2,128,128]{0,3,2,1:T(8,128)} copy(f32[3,2,128,128]{3,2,1,0:T(8,128)S(1)} %get-tuple-element.109) | data formatting | bytes 786432 | tf_op jit(solution)/shard_map/jvp()/slice | solution.py:133
  123.5 16.5 %gather_fusion = f32[4096,3]{1,0:T(8,128)S(1)} fusion(f32[3,32768]{0,1:T(8,128)} %bitcast.414, s32[4096]{0:T(1024)S(1)} %get-tuple-element.72), kind=kCustom, calls=%fused_computation | custom fusion | bytes 114688 | tf_op jit(solution)/shard_map/jvp()/gather | solution.py:168
  140.0 40.6 %gather_fusion.3 = f32[4096]{0:T(1024)} fusion(f32[32768]{0:T(1024)S(1)} %bitcast.407, s32[4096]{0:T(1024)S(1)} %get-tuple-element.72), kind=kCustom, calls=%fused_computation.3 | custom fusion | bytes 49152 | tf_op jit(solution)/shard_map/jvp()/gather | solution.py:168
  180.6 23.0 %gather_fusion.1 = f32[4096]{0:T(1024)S(1)} fusion(f32[32768]{0:T(1024)S(1)} %bitcast.408, s32[4096]{0:T(1024)S(1)} %get-tuple-element.72), kind=kCustom, calls=%fused_computation.1 | custom fusion | bytes 49152 | tf_op jit(solution)/shard_map/jvp()/gather | solution.py:168
  203.7 36.5 %scatter_custom_fusion = f32[3,32768]{0,1:T(8,128)} fusion(f32[3,32768]{0,1:T(8,128)} %bitcast.409, s32[4096]{0:T(1024)} %bitcast.429, f32[4096,3]{1,0:T(8,128)S(1)} %gather_fusion, f32[4096]{0:T(1024)S(1)} %bitcast.419, f32[4096]{0:T(1024)S(1)} %bitcast.417), kind=kCustom, calls=%fused_computation.15 | custom fusion | flops 36864 | bytes 475136 | tf_op jit(solution)/shard_map/jvp()/scatter-add | solution.py:172
  240.2 10.7 %copy.115 = f32[3,2,128,128]{3,2,1,0:T(8,128)} copy(f32[3,2,128,128]{0,3,2,1:T(8,128)} %bitcast.410) | data formatting | bytes 786432
  250.8 2.5 fusion.31
  253.3 9.5 %copy.111 = f32[3,2,128,128]{0,3,2,1:T(8,128)} copy(f32[3,2,128,128]{3,2,1,0:T(8,128)} %fusion.31) | data formatting | bytes 786432 | tf_op jit(solution)/shard_map/jvp()/sub | solution.py:163
  262.9 8.6 %copy.112 = f32[3,2,128,128]{0,3,2,1:T(8,128)} copy(f32[3,2,128,128]{3,2,1,0:T(8,128)S(1)} %get-tuple-element.108) | data formatting | bytes 786432 | tf_op jit(solution)/shard_map/jvp()/slice | solution.py:133
  271.4 20.0 %gather_fusion.2 = f32[4096,3]{1,0:T(8,128)} fusion(f32[3,32768]{0,1:T(8,128)} %bitcast.415, s32[4096]{0:T(1024)S(1)} %get-tuple-element.72), kind=kCustom, calls=%fused_computation.2 | custom fusion | bytes 114688 | tf_op jit(solution)/shard_map/jvp()/gather | solution.py:168
  291.4 37.0 %scatter_custom_fusion.1 = f32[3,32768]{0,1:T(8,128)} fusion(f32[3,32768]{0,1:T(8,128)} %bitcast.411, s32[4096]{0:T(1024)} %bitcast.430, f32[4096,3]{1,0:T(8,128)} %gather_fusion.2, f32[4096,3]{1,0:T(8,128)S(1)} %gather_fusion, f32[4096]{0:T(1024)S(1)} %bitcast.425, f32[4096]{0:T(1024)S(1)} %bitcast.420, f32[4096]{0:T(1024)S(1)} %bitcast.418), kind=kCustom, calls=%fused_computation.13 | custom fusion | flops 73728 | bytes 2588672 | tf_op jit(solution)/shard_map/jvp()/scatter-add | solution.py:172
  328.4 10.6 %copy.116 = f32[3,2,128,128]{3,2,1,0:T(8,128)} copy(f32[3,2,128,128]{0,3,2,1:T(8,128)} %bitcast.412) | data formatting | bytes 786432
  339.0 4.6 %add_reduce_fusion = (f32[32,128]{1,0:T(8,128)S(1)}, f32[32,128]{1,0:T(8,128)S(1)}, f32[3,32]{0,1:T(8,128)S(1)}) fusion(f32[3,32,128]{0,2,1:T(8,128)} %bitcast.416, f32[3,32,128]{0,2,1:T(8,128)S(1)} %bitcast.413, f32[32,128]{1,0:T(8,128)S(1)} %get-tuple-element.116, f32[32,128]{1,0:T(8,128)S(1)} %get-tuple-element.117, f32[32,128]{1,0:T(8,128)S(1)} %and_select_fusion, ...), kind=kLoop, calls=%fused_computation.17 | loop fusion | flops 126880 | bytes 229760 | tf_op jit(solution)/shard_map/reduce_sum | solution.py:181
  343.9 45.6 %all-reduce.4 = (f32[32,128]{1,0:T(8,128)S(1)}, f32[32,128]{1,0:T(8,128)S(1)}, f32[3,128]{1,0:T(4,128)S(1)}) all-reduce(f32[32,128]{1,0:T(8,128)S(1)} %get-tuple-element.55, f32[32,128]{1,0:T(8,128)S(1)} %get-tuple-element.54, f32[3,128]{1,0:T(4,128)S(1)} %fusion.157), channel_id=1, replica_groups=mesh['gx'=16,'gy'=16] {'gy'}, use_global_device_ids=true, to_apply=%region_3.4 | all-reduce | flops 8576 | bytes 68608 | tf_op jit(solution)/shard_map/psum | solution.py:201
  389.5 1.7 fusion.175
  391.4 1.7 fusion.174
  393.3 32.3 %all-reduce.5 = (f32[128]{0:T(128)S(1)}, f32[3,128]{1,0:T(4,128)}) all-reduce(f32[128]{0:T(128)S(1)} %copy-done.15, f32[3,128]{1,0:T(4,128)S(1)} %get-tuple-element.59), channel_id=1, replica_groups=mesh['gx'=16,'gy'=16] {'gx'}, use_global_device_ids=true, to_apply=%region_5.6 | all-reduce | flops 512 | bytes 4096 | tf_op jit(solution)/shard_map/psum | solution.py:187
  (112 shorter events, 26.5 us)
Async XLA Ops:
  0.6 425.2 %copy-start = (f32[128]{0:T(128)S(1)}, f32[128]{0:T(128)}, u32[]{:S(2)}) copy-start(f32[128]{0:T(128)} %param.37) | copy-start | bytes 1540
  0.6 10.9 %copy-start.8 = (s32[32,128]{1,0:T(8,128)S(1)}, s32[32,128]{1,0:T(8,128)}, u32[]{:S(2)}) copy-start(s32[32,128]{1,0:T(8,128)} %param.29) | copy-start | bytes 49156
  0.7 11.5 %copy-start.12 = (f32[32,128]{1,0:T(8,128)S(1)}, f32[32,128]{1,0:T(8,128)}, u32[]{:S(2)}) copy-start(f32[32,128]{1,0:T(8,128)} %param.30) | copy-start | bytes 49156
  0.7 11.5 %copy-start.9 = (s32[32,128]{1,0:T(8,128)S(1)}, s32[32,128]{1,0:T(8,128)}, u32[]{:S(2)}) copy-start(s32[32,128]{1,0:T(8,128)} %param.31) | copy-start | bytes 49156
  5.6 12.7 %collective-permute-start.1 = (f32[8,2,1,128]{3,2,1,0:T(1,128)S(1)}, f32[8,2,1,128]{3,2,1,0:T(1,128)S(1)}, u32[]{:S(2)}, u32[]{:S(2)}) collective-permute-start(f32[8,2,1,128]{3,2,1,0:T(1,128)S(1)} %get-tuple-element.92), channel_id=1, source_target_pairs={{16,0},{32,16},{48,32},{64,48},{80,64},{96,80},{112,96},{128,112},... | collective-permute-start | bytes 24584 | tf_op jit(solution)/shard_map/ppermute | solution.py:24
  6.9 11.4 %collective-permute-start = (f32[8,2,1,128]{3,2,1,0:T(1,128)S(1)}, f32[8,2,1,128]{3,2,1,0:T(1,128)S(1)}, u32[]{:S(2)}, u32[]{:S(2)}) collective-permute-start(f32[8,2,1,128]{3,2,1,0:T(1,128)S(1)} %get-tuple-element.91), channel_id=1, source_target_pairs={{0,16},{16,32},{32,48},{48,64},{64,80},{80,96},{96,112},{112,128},... | collective-permute-start | bytes 24584 | tf_op jit(solution)/shard_map/ppermute | solution.py:23
  15.0 2.0 copy-start.17
  15.0 2.0 copy-start.19
  15.0 2.7 copy-start.2
  18.8 8.5 %copy-start.1 = (f32[32,128]{1,0:T(8,128)S(1)}, f32[32,128]{1,0:T(8,128)}, u32[]{:S(2)}) copy-start(f32[32,128]{1,0:T(8,128)} %param.28) | copy-start | bytes 49156
  19.4 77.5 %collective-permute-start.3 = (f32[8,2,130,1]{2,0,3,1:T(8,128)S(1)}, f32[8,2,130,1]{2,0,3,1:T(8,128)S(1)}, u32[]{:S(2)}, u32[]{:S(2)}) collective-permute-start(f32[8,2,130,1]{2,0,3,1:T(8,128)S(1)} %copy.106), channel_id=1, source_target_pairs={{1,0},{2,1},{3,2},{4,3},{5,4},{6,5},{7,6},{8,7},{9,8},{10,9},{11,1... | collective-permute-start | bytes 24968 | tf_op jit(solution)/shard_map/ppermute | solution.py:24
  25.1 72.2 %collective-permute-start.2 = (f32[8,2,130,1]{2,0,3,1:T(8,128)S(1)}, f32[8,2,130,1]{2,0,3,1:T(8,128)S(1)}, u32[]{:S(2)}, u32[]{:S(2)}) collective-permute-start(f32[8,2,130,1]{2,0,3,1:T(8,128)S(1)} %copy.105), channel_id=1, source_target_pairs={{0,1},{1,2},{2,3},{3,4},{4,5},{5,6},{6,7},{7,8},{8,9},{9,10},{10,1... | collective-permute-start | bytes 24968 | tf_op jit(solution)/shard_map/ppermute | solution.py:23
  104.2 1.8 copy-start.6
  180.6 23.0 %copy-start.11 = (f32[4096]{0:T(1024)S(1)}, f32[4096]{0:T(1024)}, u32[]{:S(2)}) copy-start(f32[4096]{0:T(1024)} %gather_fusion.3) | copy-start | bytes 49156
  240.2 10.7 %copy-start.4 = (f32[3,1,128,128]{3,2,1,0:T(8,128)S(1)}, f32[3,1,128,128]{3,2,1,0:T(8,128)}, u32[]{:S(2)}) copy-start(f32[3,1,128,128]{3,2,1,0:T(8,128)} %get-tuple-element.115) | copy-start | bytes 589828
  339.0 4.7 %copy-start.18 = (s32[32,1]{0,1:T(1,128)S(1)}, s32[32,1]{0,1:T(1,128)}, u32[]{:S(2)}) copy-start(s32[32,1]{0,1:T(1,128)} %param.36) | copy-start | bytes 388
  339.0 50.5 %copy-start.3 = (bf16[32,128,128]{2,1,0:T(8,128)(2,1)S(1)}, bf16[32,128,128]{2,1,0:T(8,128)(2,1)}, u32[]{:S(2)}) copy-start(bf16[32,128,128]{2,1,0:T(8,128)(2,1)} %minimum_convert_fusion) | copy-start | bytes 3145732
  339.0 52.4 %copy-start.10 = (f32[4096]{0:T(1024)S(1)}, f32[4096]{0:T(1024)}, u32[]{:S(2)}) copy-start(f32[4096]{0:T(1024)} %gather_fusion.5) | copy-start | bytes 49156
  343.6 49.6 %copy-start.15 = (f32[128]{0:T(128)S(1)}, f32[128]{0:T(128)}, u32[]{:S(2)}) copy-start(f32[128]{0:T(128)} %convolution_bitcast_fusion.1) | copy-start | bytes 1540
  343.6 82.2 %copy-start.14 = (f32[32]{0:T(128)S(1)}, f32[32]{0:T(128)}, u32[]{:S(2)}) copy-start(f32[32]{0:T(128)} %slice_reduce_fusion.2) | copy-start | bytes 388
  343.6 82.2 %copy-start.16 = (s32[32]{0:T(128)S(1)}, s32[32]{0:T(128)}, u32[]{:S(2)}) copy-start(s32[32]{0:T(128)} %param.33) | copy-start | bytes 388
  343.7 82.2 %copy-start.20 = (f32[32]{0:T(128)S(1)}, f32[32]{0:T(128)}, u32[]{:S(2)}) copy-start(f32[32]{0:T(128)} %param.35) | copy-start | bytes 388
  343.7 82.2 %copy-start.21 = (f32[32]{0:T(128)S(1)}, f32[32]{0:T(128)}, u32[]{:S(2)}) copy-start(f32[32]{0:T(128)} %param.34) | copy-start | bytes 388
  343.7 82.4 %copy-start.13 = (f32[32,128]{1,0:T(8,128)S(1)}, f32[32,128]{1,0:T(8,128)}, u32[]{:S(2)}) copy-start(f32[32,128]{1,0:T(8,128)} %param.32) | copy-start | bytes 49156
  (2 other events, 3.0 us)
